TPU v7x, 32 devices: a whole 2x2x4 slice. The times are simulated.
32 devices in a mesh: ctx: 4 (over y, x), fsdp: 8 (over z, core).
Axes of the slice: x: 2, y: 2, z: 4, core: 2. Of those that a mesh axis runs over, the one named last changes fastest.
Arguments:
- block_pos: int32 [2, 4], P(None, 'ctx'), may hold values from 0 to 3, each once within a row
- queries: bfloat16 [8, 512, 640], P('fsdp', 'ctx'), may hold values from -6 to 6
- keys: bfloat16 [8, 512, 128], P('fsdp', 'ctx'), may hold values from -6 to 6
- values: bfloat16 [8, 512, 128], P('fsdp', 'ctx'), may hold values from -12 to 12
- attention_output: bfloat16 [8, 512, 640], P('fsdp', 'ctx'), may hold values from -6 to 6
- output_gradient: bfloat16 [8, 512, 640], P('fsdp', 'ctx'), may hold values from -24 to 24
- log_softmax_norm: float32 [8, 5, 512], P('fsdp', None, 'ctx'), may hold values from 6 to 9
- features: bfloat16 [2, 512, 2560], P(None, 'ctx', 'fsdp'), may hold values from -0.119628906 to 0.119628906
Outputs:
- grad_q: bfloat16 [8, 512, 640], P('fsdp', 'ctx')
- key_gradient: bfloat16 [8, 512, 128], P('fsdp', 'ctx')
- value_gradient: bfloat16 [8, 512, 128], P('fsdp', 'ctx')
- grad_wk: float32 [2560, 512], P('fsdp')
Inputs may be any that keep to these rules, and one draw needn't show every extreme that they name: Each row of block_pos holds every block place 0 to 3 once.
All inputs are finite; a program needn't handle non-finite values.
Results may differ from a plain program's by a relative error of at most 0.0058.
Values may be sent and summed in bfloat16 or wider, within the bound.
A program may use at most 64 MiB of HBM per device.

v0:
```python
import jax
import jax.numpy as jnp
from jax import lax
from jax.sharding import PartitionSpec as P

QUERY_HEADS = 20
KEY_VALUE_HEADS = 4
HEAD_SIZE = 128
HEAD_GROUPS = 4


def from_behind(value, axis, steps):
    count = lax.axis_size(axis)
    pairs = [(source, (source + steps) % count) for source in range(count)]
    return lax.ppermute(value, axis, pairs)


def shortened(shard):

    def short(part):
        return part.astype(jnp.bfloat16) if part.dtype == jnp.float32 else part

    return jax.tree.map(short, shard)


def block_grads(
    heads_of_queries,
    head_gradient,
    delta_heads,
    heads_of_norm,
    block_of_keys,
    block_of_values,
    key_place,
    key_offset,
    own_place,
):
    query_rows = heads_of_queries.shape[0]
    key_rows = block_of_keys.shape[0]
    score_scale = heads_of_queries.shape[-1] ** (-0.5)
    query_pos = own_place * query_rows + lax.iota(jnp.int32, query_rows)
    key_pos = key_place[0] * query_rows + key_offset + lax.iota(jnp.int32, key_rows)
    visible = key_pos[None, :] <= query_pos[:, None]
    scores = (
        jnp.einsum(
            "tkgd,ukd->kgtu", heads_of_queries, block_of_keys, preferred_element_type=jnp.float32
        )
        * score_scale
    )
    soft_probs = jnp.where(visible, jnp.exp(scores - heads_of_norm[..., None]), 0.0)
    dprobs = jnp.einsum(
        "tkgd,ukd->kgtu", head_gradient, block_of_values, preferred_element_type=jnp.float32
    )
    dscores = (soft_probs * (dprobs - delta_heads[..., None]) * score_scale).astype(jnp.bfloat16)
    probs_low = soft_probs.astype(jnp.bfloat16)
    grad_query = jnp.einsum(
        "kgtu,ukd->tkgd", dscores, block_of_keys, preferred_element_type=jnp.float32
    )
    gradient_for_key = jnp.einsum(
        "kgtu,tkgd->ukd", dscores, heads_of_queries, preferred_element_type=jnp.float32
    )
    gradient_for_value = jnp.einsum(
        "kgtu,tkgd->ukd", probs_low, head_gradient, preferred_element_type=jnp.float32
    )
    return (grad_query, gradient_for_key, gradient_for_value)


def local(
    block_pos, queries, keys, values, attention_output, output_gradient, log_softmax_norm, features
):
    rows_per_block = queries.shape[1]
    group_size = QUERY_HEADS // KEY_VALUE_HEADS
    kv_local = keys.shape[-1] // HEAD_SIZE
    sequence_index = lax.axis_index("fsdp") // HEAD_GROUPS
    own_row = lax.dynamic_slice_in_dim(block_pos, sequence_index, 1, 0)
    own_place = own_row[0, 0]
    key_place = own_row[0, 0:1]
    heads_of_queries = queries[0].reshape(rows_per_block, kv_local, group_size, HEAD_SIZE)
    head_gradient = output_gradient[0].reshape(rows_per_block, kv_local, group_size, HEAD_SIZE)
    heads_of_output = attention_output[0].reshape(rows_per_block, kv_local, group_size, HEAD_SIZE)
    delta = jnp.sum(
        head_gradient.astype(jnp.float32) * heads_of_output.astype(jnp.float32), axis=-1
    )
    delta_heads = jnp.transpose(delta, (1, 2, 0))
    heads_of_norm = log_softmax_norm[0].reshape(kv_local, group_size, rows_per_block)
    block_of_keys = keys[0].reshape(rows_per_block, kv_local, HEAD_SIZE)
    block_of_values = values[0].reshape(rows_per_block, kv_local, HEAD_SIZE)
    cycle_length = lax.axis_size("ctx")
    zero_key_gradient = jnp.zeros((rows_per_block, kv_local, HEAD_SIZE), jnp.float32)
    zero_query_gradient = jnp.zeros((rows_per_block, kv_local, group_size, HEAD_SIZE), jnp.float32)

    def visit_rows(query_acc, blocks, grad_pair, key_offset):
        add_query, add_key, add_value = block_grads(
            heads_of_queries,
            head_gradient,
            delta_heads,
            heads_of_norm,
            blocks[0],
            blocks[1],
            blocks[2],
            key_offset,
            own_place,
        )
        return (query_acc + add_query, (grad_pair[0] + add_key, grad_pair[1] + add_value))

    def visit(query_acc, blocks, grad_pair):
        return visit_rows(query_acc, blocks, grad_pair, 0)

    def pass_grads(grad_pair):
        return from_behind(grad_pair, "ctx", 1)

    def cycle_step(step_index, cycle_state):
        query_acc, blocks, grad_pair = cycle_state
        query_acc, grad_pair = visit(query_acc, blocks, grad_pair)
        blocks = jax.tree.map(
            lambda part, own: part.astype(own.dtype),
            from_behind(shortened(blocks), "ctx", 1),
            blocks,
        )
        grad_pair = pass_grads(grad_pair)
        return (query_acc, blocks, grad_pair)

    cycle_state = (
        zero_query_gradient,
        (block_of_keys, block_of_values, key_place),
        (zero_key_gradient, zero_key_gradient),
    )
    query_acc, blocks, grad_pair = lax.fori_loop(0, cycle_length - 1, cycle_step, cycle_state)
    query_acc, grad_pair = visit(query_acc, blocks, grad_pair)
    grad_pair = pass_grads(grad_pair)
    key_gradient_sum = grad_pair[0]
    value_gradient_sum = grad_pair[1]
    grad_q = query_acc.reshape(rows_per_block, -1).astype(jnp.bfloat16)
    key_gradient = key_gradient_sum.reshape(rows_per_block, -1).astype(jnp.bfloat16)
    value_gradient = value_gradient_sum.reshape(rows_per_block, -1).astype(jnp.bfloat16)
    local_width = key_gradient.shape[-1]
    feature_cols = features.shape[-1]
    piece = lax.all_gather(key_gradient[None], "fsdp", axis=0, tiled=True)
    count = piece.shape[0]
    indices = lax.iota(jnp.int32, count)
    seq_ids = indices // HEAD_GROUPS
    group_ids = indices % HEAD_GROUPS
    chosen = jnp.take(features, seq_ids, axis=0)
    contrib = jnp.einsum("pti,ptj->pij", chosen, piece, preferred_element_type=jnp.float32)
    rounded = lax.optimization_barrier(contrib.astype(jnp.bfloat16)).astype(jnp.float32)
    placing = (group_ids[:, None] == lax.iota(jnp.int32, HEAD_GROUPS)[None, :]).astype(jnp.float32)
    summed = jnp.einsum("pij,pr->irj", rounded, placing)
    summed = summed.reshape(feature_cols, HEAD_GROUPS * local_width)
    share = lax.psum_scatter(summed, "ctx", scatter_dimension=1, tiled=True)
    grad_wk = lax.all_gather(share, "ctx", axis=1, tiled=True)
    return (grad_q[None], key_gradient[None], value_gradient[None], grad_wk)


def solution(mesh):
    return jax.shard_map(
        local,
        mesh=mesh,
        in_specs=(
            P(None, "ctx"),
            P("fsdp", "ctx", None),
            P("fsdp", "ctx", None),
            P("fsdp", "ctx", None),
            P("fsdp", "ctx", None),
            P("fsdp", "ctx", None),
            P("fsdp", None, "ctx"),
            P(None, "ctx", "fsdp"),
        ),
        out_specs=(
            P("fsdp", "ctx", None),
            P("fsdp", "ctx", None),
            P("fsdp", "ctx", None),
            P("fsdp", None),
        ),
        check_vma=False,
    )
```

profile of v0, /device:TPU:0, one launch (start us, length us, event | category | flops | bytes accessed | tf_op | source)
XLA Modules:
  0.0 129.1 jit_solution(5802432988450264913)
XLA Ops:
  12.6 43.1 %while.23 = (s32[]{:T(128)}, f32[128,1,5,128]{3,0,2,1:T(8,128)S(1)}, bf16[128,1,128]{2,0,1:T(8,128)(2,1)S(1)}, bf16[128,1,128]{2,0,1:T(8,128)(2,1)S(1)}, s32[1]{...) while((s32[]{:T(128)}, ...), condition=%wide.region_2.3_spmd.clone, body=%wide.region_1.2_spmd.clone.sunk | while | flops 105726208 | bytes 4103563 | solution.py:127
  13.3 4.3 %collective-permute-start.2 = (s32[1]{0:T(128)}, s32[1]{0:T(128)}, u32[]{:S(2)}, u32[]{:S(2)}) collective-permute-start(s32[1]{0:T(128)} %copy.68), channel_id=1, source_target_pairs={{0,8},{8,16},{16,24},{24,0},{1,9},{9,17},{17,25},{25,1},{2,10},{10... | collective-permute-start | bytes 20 | tf_op jit(solution)/shard_map/while/body/eval_jaxpr/ppermute | solution.py:15
  17.5 1.5 %collective-permute-start.1 = (bf16[128,1,128]{2,0,1:T(8,128)(2,1)S(1)}, bf16[128,1,128]{2,0,1:T(8,128)(2,1)S(1)}, u32[]{:S(2)}, u32[]{:S(2)}) collective-permute-start(bf16[128,1,128]{2,0,1:T(8,128)(2,1)S(1)} %copy.67), channel_id=1, source_target_pairs={{0,8},{8,16},{16,24},{24,0},{1,9},{9,17},{17,25},{25,1},{2,10},{10... | collective-permute-start | bytes 98312 | tf_op jit(solution)/shard_map/while/body/eval_jaxpr/ppermute | solution.py:15
  19.0 1.5 %collective-permute-start = (bf16[128,1,128]{2,0,1:T(8,128)(2,1)S(1)}, bf16[128,1,128]{2,0,1:T(8,128)(2,1)S(1)}, u32[]{:S(2)}, u32[]{:S(2)}) collective-permute-start(bf16[128,1,128]{2,0,1:T(8,128)(2,1)S(1)} %copy.66), channel_id=1, source_target_pairs={{0,8},{8,16},{16,24},{24,0},{1,9},{9,17},{17,25},{25,1},{2,10},{10... | collective-permute-start | bytes 98312 | tf_op jit(solution)/shard_map/while/body/eval_jaxpr/ppermute | solution.py:15
  22.2 2.0 %collective-permute-start.4 = (f32[128,1,128]{2,0,1:T(8,128)S(1)}, f32[128,1,128]{2,0,1:T(8,128)S(1)}, u32[]{:S(2)}, u32[]{:S(2)}) collective-permute-start(f32[128,1,128]{2,0,1:T(8,128)S(1)} %fusion.90), channel_id=1, source_target_pairs={{0,8},{8,16},{16,24},{24,0},{1,9},{9,17},{17,25},{25,1},{2,10},{10... | collective-permute-start | bytes 196616 | tf_op jit(solution)/shard_map/while/body/eval_jaxpr/ppermute | solution.py:15
  24.5 2.6 %collective-permute-done.3 = f32[128,1,128]{2,0,1:T(8,128)S(1)} collective-permute-done((f32[128,1,128]{2,0,1:T(8,128)S(1)}, f32[128,1,128]{2,0,1:T(8,128)S(1)}, u32[]{:S(2)}, u32[]{:S(2)}) %collective-permute-start.3) | collective-permute-done | bytes 65568 | tf_op jit(solution)/shard_map/while/body/eval_jaxpr/ppermute | solution.py:15
  28.5 2.0 %collective-permute-start.2 = (s32[1]{0:T(128)}, s32[1]{0:T(128)}, u32[]{:S(2)}, u32[]{:S(2)}) collective-permute-start(s32[1]{0:T(128)} %copy.68), channel_id=1, source_target_pairs={{0,8},{8,16},{16,24},{24,0},{1,9},{9,17},{17,25},{25,1},{2,10},{10... | collective-permute-start | bytes 20 | tf_op jit(solution)/shard_map/while/body/eval_jaxpr/ppermute | solution.py:15
  30.4 2.4 %collective-permute-start.1 = (bf16[128,1,128]{2,0,1:T(8,128)(2,1)S(1)}, bf16[128,1,128]{2,0,1:T(8,128)(2,1)S(1)}, u32[]{:S(2)}, u32[]{:S(2)}) collective-permute-start(bf16[128,1,128]{2,0,1:T(8,128)(2,1)S(1)} %copy.67), channel_id=1, source_target_pairs={{0,8},{8,16},{16,24},{24,0},{1,9},{9,17},{17,25},{25,1},{2,10},{10... | collective-permute-start | bytes 98312 | tf_op jit(solution)/shard_map/while/body/eval_jaxpr/ppermute | solution.py:15
  34.8 1.4 %collective-permute-start.3 = (f32[128,1,128]{2,0,1:T(8,128)S(1)}, f32[128,1,128]{2,0,1:T(8,128)S(1)}, u32[]{:S(2)}, u32[]{:S(2)}) collective-permute-start(f32[128,1,128]{2,0,1:T(8,128)S(1)} %fusion.89), channel_id=1, source_target_pairs={{0,8},{8,16},{16,24},{24,0},{1,9},{9,17},{17,25},{25,1},{2,10},{10... | collective-permute-start | bytes 196616 | tf_op jit(solution)/shard_map/while/body/eval_jaxpr/ppermute | solution.py:15
  37.6 2.4 %collective-permute-done.3 = f32[128,1,128]{2,0,1:T(8,128)S(1)} collective-permute-done((f32[128,1,128]{2,0,1:T(8,128)S(1)}, f32[128,1,128]{2,0,1:T(8,128)S(1)}, u32[]{:S(2)}, u32[]{:S(2)}) %collective-permute-start.3) | collective-permute-done | bytes 65568 | tf_op jit(solution)/shard_map/while/body/eval_jaxpr/ppermute | solution.py:15
  40.0 2.0 %collective-permute-done.4 = f32[128,1,128]{2,0,1:T(8,128)S(1)} collective-permute-done((f32[128,1,128]{2,0,1:T(8,128)S(1)}, f32[128,1,128]{2,0,1:T(8,128)S(1)}, u32[]{:S(2)}, u32[]{:S(2)}) %collective-permute-start.4) | collective-permute-done | bytes 65568 | tf_op jit(solution)/shard_map/while/body/eval_jaxpr/ppermute | solution.py:15
  42.6 1.4 %collective-permute-start.2 = (s32[1]{0:T(128)}, s32[1]{0:T(128)}, u32[]{:S(2)}, u32[]{:S(2)}) collective-permute-start(s32[1]{0:T(128)} %copy.68), channel_id=1, source_target_pairs={{0,8},{8,16},{16,24},{24,0},{1,9},{9,17},{17,25},{25,1},{2,10},{10... | collective-permute-start | bytes 20 | tf_op jit(solution)/shard_map/while/body/eval_jaxpr/ppermute | solution.py:15
  44.0 3.0 %collective-permute-start.1 = (bf16[128,1,128]{2,0,1:T(8,128)(2,1)S(1)}, bf16[128,1,128]{2,0,1:T(8,128)(2,1)S(1)}, u32[]{:S(2)}, u32[]{:S(2)}) collective-permute-start(bf16[128,1,128]{2,0,1:T(8,128)(2,1)S(1)} %copy.67), channel_id=1, source_target_pairs={{0,8},{8,16},{16,24},{24,0},{1,9},{9,17},{17,25},{25,1},{2,10},{10... | collective-permute-start | bytes 98312 | tf_op jit(solution)/shard_map/while/body/eval_jaxpr/ppermute | solution.py:15
  48.4 2.0 %collective-permute-start.3 = (f32[128,1,128]{2,0,1:T(8,128)S(1)}, f32[128,1,128]{2,0,1:T(8,128)S(1)}, u32[]{:S(2)}, u32[]{:S(2)}) collective-permute-start(f32[128,1,128]{2,0,1:T(8,128)S(1)} %fusion.89), channel_id=1, source_target_pairs={{0,8},{8,16},{16,24},{24,0},{1,9},{9,17},{17,25},{25,1},{2,10},{10... | collective-permute-start | bytes 196616 | tf_op jit(solution)/shard_map/while/body/eval_jaxpr/ppermute | solution.py:15
  51.8 2.1 %collective-permute-done.3 = f32[128,1,128]{2,0,1:T(8,128)S(1)} collective-permute-done((f32[128,1,128]{2,0,1:T(8,128)S(1)}, f32[128,1,128]{2,0,1:T(8,128)S(1)}, u32[]{:S(2)}, u32[]{:S(2)}) %collective-permute-start.3) | collective-permute-done | bytes 65568 | tf_op jit(solution)/shard_map/while/body/eval_jaxpr/ppermute | solution.py:15
  53.8 1.9 %collective-permute-done.4 = f32[128,1,128]{2,0,1:T(8,128)S(1)} collective-permute-done((f32[128,1,128]{2,0,1:T(8,128)S(1)}, f32[128,1,128]{2,0,1:T(8,128)S(1)}, u32[]{:S(2)}, u32[]{:S(2)}) %collective-permute-start.4) | collective-permute-done | bytes 65568 | tf_op jit(solution)/shard_map/while/body/eval_jaxpr/ppermute | solution.py:15
  58.6 4.1 %collective-permute-done.5 = bf16[128,1,128]{2,0,1:T(8,128)(2,1)S(1)} collective-permute-done((bf16[128,1,128]{2,0,1:T(8,128)(2,1)S(1)}, bf16[128,1,128]{2,0,1:T(8,128)(2,1)S(1)}, u32[]{:S(2)}, u32[]{:S(2)}) %collective-permute-start.5) | collective-permute-done | bytes 32800 | tf_op jit(solution)/shard_map/ppermute | solution.py:15
  62.6 14.4 %all-gather = bf16[1024,1,128]{2,0,1:T(8,128)(2,1)S(1)} all-gather(bf16[128,1,128]{2,0,1:T(8,128)(2,1)S(1)} %collective-permute-done.5), channel_id=2, replica_groups=mesh['ctx'=4,'fsdp'=8] {'fsdp'}, dimensions={0}, use_global_device_ids=true | all-gather | bytes 294912 | tf_op jit(solution)/shard_map/all_gather | solution.py:137
  78.2 0.9 copy.55
  79.8 0.8 copy.38
  80.6 3.6 %collective-permute-done.6 = bf16[128,1,128]{2,0,1:T(8,128)(2,1)S(1)} collective-permute-done((bf16[128,1,128]{2,0,1:T(8,128)(2,1)S(1)}, bf16[128,1,128]{2,0,1:T(8,128)(2,1)S(1)}, u32[]{:S(2)}, u32[]{:S(2)}) %collective-permute-start.6) | collective-permute-done | bytes 32800 | tf_op jit(solution)/shard_map/ppermute | solution.py:15
  84.2 20.7 %reduce-scatter.2.cloned.1.call-done = f32[320,128]{1,0:T(8,128)} async-done(((f32[320,512]{1,0:T(8,128)}), f32[320,128]{1,0:T(8,128)}) %reduce-scatter.2.cloned.1.call-update) | async-done | bytes 163856 | tf_op jit(solution)/shard_map/reduce_scatter | solution.py:148
  104.8 15.4 %all_gather.7 = f32[320,512]{1,0:T(8,128)S(1)} all-gather(f32[320,128]{1,0:T(8,128)} %reduce-scatter.2.cloned.1.call-done), channel_id=1, replica_groups=mesh['ctx'=4,'fsdp'=8] {'ctx'}, dimensions={1}, use_global_device_ids=true | all-gather | bytes 819200 | tf_op jit(solution)/shard_map/all_gather | solution.py:149
  121.4 0.8 copy.87
  (94 shorter events, 19.3 us)
Async XLA Ops:
  7.2 50.7 %copy-start = (bf16[2,128,320]{1,2,0:T(8,128)(2,1)S(1)}, bf16[2,128,320]{1,2,0:T(8,128)(2,1)}, u32[]{:S(2)}) copy-start(bf16[2,128,320]{1,2,0:T(8,128)(2,1)} %param.17) | copy-start | bytes 491524
  7.2 1.0 copy-start.3
  7.2 97.7 %reduce-scatter.2.cloned.1.call-start = ((), (), s32[]{:S(2)}) async-start(), calls=%async_computation.1 | async-start | bytes 819200 | tf_op jit(solution)/shard_map/reduce_scatter | solution.py:148
  8.1 0.9 copy-start.4
  9.4 0.9 copy-start.5
  11.9 0.8 copy-start.1
  11.9 0.8 copy-start.2
  13.3 11.2 %collective-permute-start.2 = (s32[1]{0:T(128)}, s32[1]{0:T(128)}, u32[]{:S(2)}, u32[]{:S(2)}) collective-permute-start(s32[1]{0:T(128)} %copy.68), channel_id=1, source_target_pairs={{0,8},{8,16},{16,24},{24,0},{1,9},{9,17},{17,25},{25,1},{2,10},{10... | collective-permute-start | bytes 20 | tf_op jit(solution)/shard_map/while/body/eval_jaxpr/ppermute | solution.py:15
  17.5 6.9 %collective-permute-start.1 = (bf16[128,1,128]{2,0,1:T(8,128)(2,1)S(1)}, bf16[128,1,128]{2,0,1:T(8,128)(2,1)S(1)}, u32[]{:S(2)}, u32[]{:S(2)}) collective-permute-start(bf16[128,1,128]{2,0,1:T(8,128)(2,1)S(1)} %copy.67), channel_id=1, source_target_pairs={{0,8},{8,16},{16,24},{24,0},{1,9},{9,17},{17,25},{25,1},{2,10},{10... | collective-permute-start | bytes 98312 | tf_op jit(solution)/shard_map/while/body/eval_jaxpr/ppermute | solution.py:15
  19.0 5.5 %collective-permute-start = (bf16[128,1,128]{2,0,1:T(8,128)(2,1)S(1)}, bf16[128,1,128]{2,0,1:T(8,128)(2,1)S(1)}, u32[]{:S(2)}, u32[]{:S(2)}) collective-permute-start(bf16[128,1,128]{2,0,1:T(8,128)(2,1)S(1)} %copy.66), channel_id=1, source_target_pairs={{0,8},{8,16},{16,24},{24,0},{1,9},{9,17},{17,25},{25,1},{2,10},{10... | collective-permute-start | bytes 98312 | tf_op jit(solution)/shard_map/while/body/eval_jaxpr/ppermute | solution.py:15
  21.9 5.2 %collective-permute-start.3 = (f32[128,1,128]{2,0,1:T(8,128)S(1)}, f32[128,1,128]{2,0,1:T(8,128)S(1)}, u32[]{:S(2)}, u32[]{:S(2)}) collective-permute-start(f32[128,1,128]{2,0,1:T(8,128)S(1)} %fusion.89), channel_id=1, source_target_pairs={{0,8},{8,16},{16,24},{24,0},{1,9},{9,17},{17,25},{25,1},{2,10},{10... | collective-permute-start | bytes 196616 | tf_op jit(solution)/shard_map/while/body/eval_jaxpr/ppermute | solution.py:15
  22.2 5.6 %collective-permute-start.4 = (f32[128,1,128]{2,0,1:T(8,128)S(1)}, f32[128,1,128]{2,0,1:T(8,128)S(1)}, u32[]{:S(2)}, u32[]{:S(2)}) collective-permute-start(f32[128,1,128]{2,0,1:T(8,128)S(1)} %fusion.90), channel_id=1, source_target_pairs={{0,8},{8,16},{16,24},{24,0},{1,9},{9,17},{17,25},{25,1},{2,10},{10... | collective-permute-start | bytes 196616 | tf_op jit(solution)/shard_map/while/body/eval_jaxpr/ppermute | solution.py:15
  28.5 8.9 %collective-permute-start.2 = (s32[1]{0:T(128)}, s32[1]{0:T(128)}, u32[]{:S(2)}, u32[]{:S(2)}) collective-permute-start(s32[1]{0:T(128)} %copy.68), channel_id=1, source_target_pairs={{0,8},{8,16},{16,24},{24,0},{1,9},{9,17},{17,25},{25,1},{2,10},{10... | collective-permute-start | bytes 20 | tf_op jit(solution)/shard_map/while/body/eval_jaxpr/ppermute | solution.py:15
  30.4 7.0 %collective-permute-start.1 = (bf16[128,1,128]{2,0,1:T(8,128)(2,1)S(1)}, bf16[128,1,128]{2,0,1:T(8,128)(2,1)S(1)}, u32[]{:S(2)}, u32[]{:S(2)}) collective-permute-start(bf16[128,1,128]{2,0,1:T(8,128)(2,1)S(1)} %copy.67), channel_id=1, source_target_pairs={{0,8},{8,16},{16,24},{24,0},{1,9},{9,17},{17,25},{25,1},{2,10},{10... | collective-permute-start | bytes 98312 | tf_op jit(solution)/shard_map/while/body/eval_jaxpr/ppermute | solution.py:15
  32.8 4.8 %collective-permute-start = (bf16[128,1,128]{2,0,1:T(8,128)(2,1)S(1)}, bf16[128,1,128]{2,0,1:T(8,128)(2,1)S(1)}, u32[]{:S(2)}, u32[]{:S(2)}) collective-permute-start(bf16[128,1,128]{2,0,1:T(8,128)(2,1)S(1)} %copy.66), channel_id=1, source_target_pairs={{0,8},{8,16},{16,24},{24,0},{1,9},{9,17},{17,25},{25,1},{2,10},{10... | collective-permute-start | bytes 98312 | tf_op jit(solution)/shard_map/while/body/eval_jaxpr/ppermute | solution.py:15
  34.8 5.2 %collective-permute-start.3 = (f32[128,1,128]{2,0,1:T(8,128)S(1)}, f32[128,1,128]{2,0,1:T(8,128)S(1)}, u32[]{:S(2)}, u32[]{:S(2)}) collective-permute-start(f32[128,1,128]{2,0,1:T(8,128)S(1)} %fusion.89), channel_id=1, source_target_pairs={{0,8},{8,16},{16,24},{24,0},{1,9},{9,17},{17,25},{25,1},{2,10},{10... | collective-permute-start | bytes 196616 | tf_op jit(solution)/shard_map/while/body/eval_jaxpr/ppermute | solution.py:15
  36.4 5.6 %collective-permute-start.4 = (f32[128,1,128]{2,0,1:T(8,128)S(1)}, f32[128,1,128]{2,0,1:T(8,128)S(1)}, u32[]{:S(2)}, u32[]{:S(2)}) collective-permute-start(f32[128,1,128]{2,0,1:T(8,128)S(1)} %fusion.90), channel_id=1, source_target_pairs={{0,8},{8,16},{16,24},{24,0},{1,9},{9,17},{17,25},{25,1},{2,10},{10... | collective-permute-start | bytes 196616 | tf_op jit(solution)/shard_map/while/body/eval_jaxpr/ppermute | solution.py:15
  42.6 8.3 %collective-permute-start.2 = (s32[1]{0:T(128)}, s32[1]{0:T(128)}, u32[]{:S(2)}, u32[]{:S(2)}) collective-permute-start(s32[1]{0:T(128)} %copy.68), channel_id=1, source_target_pairs={{0,8},{8,16},{16,24},{24,0},{1,9},{9,17},{17,25},{25,1},{2,10},{10... | collective-permute-start | bytes 20 | tf_op jit(solution)/shard_map/while/body/eval_jaxpr/ppermute | solution.py:15
  44.0 7.0 %collective-permute-start.1 = (bf16[128,1,128]{2,0,1:T(8,128)(2,1)S(1)}, bf16[128,1,128]{2,0,1:T(8,128)(2,1)S(1)}, u32[]{:S(2)}, u32[]{:S(2)}) collective-permute-start(bf16[128,1,128]{2,0,1:T(8,128)(2,1)S(1)} %copy.67), channel_id=1, source_target_pairs={{0,8},{8,16},{16,24},{24,0},{1,9},{9,17},{17,25},{25,1},{2,10},{10... | collective-permute-start | bytes 98312 | tf_op jit(solution)/shard_map/while/body/eval_jaxpr/ppermute | solution.py:15
  47.0 4.8 %collective-permute-start = (bf16[128,1,128]{2,0,1:T(8,128)(2,1)S(1)}, bf16[128,1,128]{2,0,1:T(8,128)(2,1)S(1)}, u32[]{:S(2)}, u32[]{:S(2)}) collective-permute-start(bf16[128,1,128]{2,0,1:T(8,128)(2,1)S(1)} %copy.66), channel_id=1, source_target_pairs={{0,8},{8,16},{16,24},{24,0},{1,9},{9,17},{17,25},{25,1},{2,10},{10... | collective-permute-start | bytes 98312 | tf_op jit(solution)/shard_map/while/body/eval_jaxpr/ppermute | solution.py:15
  48.4 5.4 %collective-permute-start.3 = (f32[128,1,128]{2,0,1:T(8,128)S(1)}, f32[128,1,128]{2,0,1:T(8,128)S(1)}, u32[]{:S(2)}, u32[]{:S(2)}) collective-permute-start(f32[128,1,128]{2,0,1:T(8,128)S(1)} %fusion.89), channel_id=1, source_target_pairs={{0,8},{8,16},{16,24},{24,0},{1,9},{9,17},{17,25},{25,1},{2,10},{10... | collective-permute-start | bytes 196616 | tf_op jit(solution)/shard_map/while/body/eval_jaxpr/ppermute | solution.py:15
  50.6 5.2 %collective-permute-start.4 = (f32[128,1,128]{2,0,1:T(8,128)S(1)}, f32[128,1,128]{2,0,1:T(8,128)S(1)}, u32[]{:S(2)}, u32[]{:S(2)}) collective-permute-start(f32[128,1,128]{2,0,1:T(8,128)S(1)} %fusion.90), channel_id=1, source_target_pairs={{0,8},{8,16},{16,24},{24,0},{1,9},{9,17},{17,25},{25,1},{2,10},{10... | collective-permute-start | bytes 196616 | tf_op jit(solution)/shard_map/while/body/eval_jaxpr/ppermute | solution.py:15
  57.8 4.9 %collective-permute-start.5 = (bf16[128,1,128]{2,0,1:T(8,128)(2,1)S(1)}, bf16[128,1,128]{2,0,1:T(8,128)(2,1)S(1)}, u32[]{:S(2)}, u32[]{:S(2)}) collective-permute-start(bf16[128,1,128]{2,0,1:T(8,128)(2,1)S(1)} %fusion.32), channel_id=1, source_target_pairs={{0,8},{8,16},{16,24},{24,0},{1,9},{9,17},{17,25},{25,1},{2,10},{10... | collective-permute-start | bytes 98312 | tf_op jit(solution)/shard_map/ppermute | solution.py:15
  79.3 4.9 %collective-permute-start.6 = (bf16[128,1,128]{2,0,1:T(8,128)(2,1)S(1)}, bf16[128,1,128]{2,0,1:T(8,128)(2,1)S(1)}, u32[]{:S(2)}, u32[]{:S(2)}) collective-permute-start(bf16[128,1,128]{2,0,1:T(8,128)(2,1)S(1)} %fusion.33), channel_id=1, source_target_pairs={{0,8},{8,16},{16,24},{24,0},{1,9},{9,17},{17,25},{25,1},{2,10},{10... | collective-permute-start | bytes 98312 | tf_op jit(solution)/shard_map/ppermute | solution.py:15
  (2 other events, 1.4 us)
Sparse Core Ops, SparseCore 0:
  79.2 25.5 reduce-scatter.1
where the time goes:
time: 129 us
  waiting for transfers between devices  41 us (32%)
  blocking collectives  29.8 us (23%)
  starting transfers between devices  23 us (18%)
  between operations  14.9 us (12%)
  local copies, waits for them, and re-layouts  9.65 us (7%)
  matrix products  5.04 us (4%)
  other arithmetic  3.66 us (3%)
  loops' own time  2.07 us (2%)
    ppermute x17, starting transfers between devices, from_behind(): return lax.ppermute(value, axis, pairs)  22.9 us
    reduce_scatter x1, waiting for transfers between devices, local(): share = lax.psum_scatter(summed, 'ctx', scatter_dimension=1, tiled=True)  20.7 us
    ppermute x17, waiting for transfers between devices, from_behind(): return lax.ppermute(value, axis, pairs)  20.4 us
    all_gather x1, blocking collectives, local(): grad_wk = lax.all_gather(share, 'ctx', axis=1, tiled=True)  15.4 us
    all_gather x1, blocking collectives, local(): piece = lax.all_gather(key_gradient[None], 'fsdp', axis=0, tiled=True)  14.4 us
    unnamed x27, local copies, waits for them, and re-layouts  8.36 us
    add x4, other arithmetic, block_grads(): query_pos = own_place * query_rows + lax.iota(jnp.int32, query_rows)  2.59 us
  transfers between devices with their start and end apart: 18, of which 11 were waited for; matrix products, arithmetic and copies ran while one was open for 6% of the time, Pallas kernels for 0%

commit v1 on v0

v1 whole, which is shorter than its diff:
```python
import functools

import jax
import jax.numpy as jnp
from jax import lax
from jax.experimental import pallas as pl
from jax.experimental.pallas import tpu as pltpu
from jax.sharding import PartitionSpec as P

QUERY_HEADS = 20
KEY_VALUE_HEADS = 4
HEAD_SIZE = 128
HEAD_GROUPS = 4
PLACE_ROWS = 16

F32 = jnp.float32
BF16 = jnp.bfloat16


def flipped(index, bits, count):
    total, unit = 0, 1
    while unit < count:
        digit = lax.rem(index // unit + (bits // unit) % 2, 2)
        total = total + digit * unit
        unit *= 2
    return total


def dot(a, b, contract):
    return lax.dot_general(a, b, ((contract[:1], contract[1:]), ((), ())), preferred_element_type=F32)


def kernel(
    n_ctx,
    n_fsdp,
    reducers,
    pos_ref,
    q_ref,
    k_ref,
    v_ref,
    o_ref,
    do_ref,
    lse_ref,
    x_ref,
    gq_ref,
    gk_ref,
    gv_ref,
    gw_ref,
    kv,
    qs,
    dos,
    ds,
    part_k,
    part_v,
    got_k,
    got_v,
    acc_k,
    acc_v,
    dk_all,
    x_t,
    rs_out,
    rs_in,
    ag_out,
    ag_in,
    kv_s,
    kv_r,
    pk_s,
    pk_r,
    pv_s,
    pv_r,
    dk_s,
    dk_r,
    rs_s,
    rs_r,
    ag_s,
    ag_r,
):
    rows = k_ref.shape[1]
    heads = q_ref.shape[2] // HEAD_SIZE
    seqs = x_ref.shape[0]
    scale = HEAD_SIZE ** (-0.5)
    c = lax.axis_index("ctx")
    f = lax.axis_index("fsdp")
    ctx_peers = {d: flipped(c, d, n_ctx) for d in range(1, n_ctx)}
    fsdp_peers = {e: flipped(f, e, n_fsdp) for e in range(1, n_fsdp)}
    direct = [e for e in range(1, n_fsdp) if e == 1 or e % 2 == 0]

    def remote(src, dst, send, recv, device):
        return pltpu.make_async_remote_copy(
            src_ref=src,
            dst_ref=dst,
            send_sem=send,
            recv_sem=recv,
            device_id=device,
            device_id_type=pl.DeviceIdType.MESH,
        )

    barrier = pltpu.get_barrier_semaphore()
    for d in range(1, n_ctx):
        pl.semaphore_signal(
            barrier, inc=1, device_id=(ctx_peers[d], f), device_id_type=pl.DeviceIdType.MESH
        )
    for e in direct:
        pl.semaphore_signal(
            barrier, inc=1, device_id=(c, fsdp_peers[e]), device_id_type=pl.DeviceIdType.MESH
        )
    place = pos_ref[f // HEAD_GROUPS, 0].astype(F32)
    kv[0, :rows] = k_ref[0]
    kv[0, rows : 2 * rows] = v_ref[0]
    kv[0, 2 * rows :] = jnp.full((PLACE_ROWS, HEAD_SIZE), place, F32).astype(BF16)
    pl.semaphore_wait(barrier, n_ctx - 1 + len(direct))

    kv_copies = {}
    for d in range(1, n_ctx):
        kv_copies[d] = remote(kv.at[0], kv.at[d], kv_s.at[d], kv_r.at[d], (ctx_peers[d], f))
        kv_copies[d].start()

    delta = []
    for h in range(heads):
        cols = slice(h * HEAD_SIZE, (h + 1) * HEAD_SIZE)
        qs[h * rows : (h + 1) * rows] = q_ref[0, :, cols]
        dos[h * rows : (h + 1) * rows] = do_ref[0, :, cols]
        product = do_ref[0, :, cols].astype(F32) * o_ref[0, :, cols].astype(F32)
        delta.append(jnp.sum(product.T, axis=0, keepdims=True))
    delta = jnp.concatenate(delta, axis=1)
    norms = lse_ref[0]
    norm = jnp.concatenate([norms[h : h + 1] for h in range(heads)], axis=1)
    token = lax.broadcasted_iota(jnp.int32, (1, rows), 1).astype(F32)
    key_row = lax.broadcasted_iota(jnp.int32, (rows, heads * rows), 0).astype(F32)

    def visit(d):
        key = kv[d, :rows]
        value = kv[d, rows : 2 * rows]
        key_place = jnp.max(kv[d, 2 * rows :].astype(F32), axis=0, keepdims=True)
        limit = token + (place - key_place) * rows
        visible = key_row <= jnp.concatenate([limit] * heads, axis=1)
        scores = dot(key, qs[...], (1, 1)) * scale
        probs = jnp.where(visible, jnp.exp(scores - norm), 0.0)
        dprobs = dot(value, dos[...], (1, 1))
        dscores = (probs * (dprobs - delta) * scale).astype(BF16)
        ds[d * rows : (d + 1) * rows] = dscores
        return dot(dscores, qs[...], (1, 0)), lambda: dot(probs.astype(BF16), dos[...], (1, 0))

    own_k, own_v = visit(0)
    acc_k[...] = own_k
    acc_v[...] = own_v()
    for s in range(seqs):
        x_t[:, s * rows : (s + 1) * rows] = x_ref[s].T

    pk_copies, pv_copies = {}, {}
    for d in range(1, n_ctx):
        kv_copies[d].wait_recv()
        to_k, to_v = visit(d)
        device = (ctx_peers[d], f)
        part_k[d] = to_k.astype(BF16)
        pk_copies[d] = remote(part_k.at[d], got_k.at[d], pk_s.at[d], pk_r.at[d], device)
        pk_copies[d].start()
        part_v[d] = to_v().astype(BF16)
        pv_copies[d] = remote(part_v.at[d], got_v.at[d], pv_s.at[d], pv_r.at[d], device)
        pv_copies[d].start()

    keys_all = jnp.concatenate([kv[d, :rows] for d in range(n_ctx)], axis=0)
    for h in range(heads):
        cols = slice(h * HEAD_SIZE, (h + 1) * HEAD_SIZE)
        gq_ref[0, :, cols] = dot(ds[:, cols], keys_all, (0, 0)).astype(BF16)

    dk = acc_k[...]
    for d in range(1, n_ctx):
        pk_copies[d].wait_recv()
        dk = dk + got_k[d].astype(F32)
    dk_low = dk.astype(BF16)
    gk_ref[0] = dk_low

    def slot(index):
        start = pl.multiple_of((index // HEAD_GROUPS) * rows, rows)
        return dk_all.at[lax.rem(index, HEAD_GROUPS), pl.ds(start, rows)]

    own_slot = slot(f)
    own_slot[...] = dk_low
    dk_copies = {}
    for e in direct:
        dk_copies[e] = remote(own_slot, own_slot, dk_s.at[e], dk_r.at[e], (c, fsdp_peers[e]))
        dk_copies[e].start()
    dv = acc_v[...]
    for d in range(1, n_ctx):
        pv_copies[d].wait_recv()
        dv = dv + got_v[d].astype(F32)
    gv_ref[0] = dv.astype(BF16)

    def arrived(e):
        there = slot(fsdp_peers[e])
        remote(there, there, dk_s.at[e], dk_r.at[e], (c, fsdp_peers[1])).wait_recv()

    for e in direct[1:]:
        arrived(e)
        there = slot(fsdp_peers[e])
        dk_copies[e + 1] = remote(
            there, there, dk_s.at[e + 1], dk_r.at[e + 1], (c, fsdp_peers[1])
        )
        dk_copies[e + 1].start()
    arrived(1)
    for e in direct[1:]:
        arrived(e + 1)

    width = gw_ref.shape[1] // reducers

    def chunk(owner):
        per = HEAD_SIZE
        groups = width // per
        parts = [dot(x_t[...], dk_all[owner * groups + g], (1, 0)) for g in range(groups)]
        return parts[0] if groups == 1 else jnp.concatenate(parts, axis=1)

    def columns(owner):
        return pl.ds(pl.multiple_of(owner * width, width), width)

    def guarded(index):
        if reducers == n_ctx:
            return lambda body: body()
        return pl.when(index < reducers)

    def rs_copy(d):
        return remote(rs_out.at[d], rs_in.at[d], rs_s.at[d], rs_r.at[d], (ctx_peers[d], f))

    def ag_copy(d):
        return remote(ag_out, ag_in.at[d], ag_s.at[d], ag_r.at[d], (ctx_peers[d], f))

    for d in range(1, n_ctx):

        @guarded(ctx_peers[d])
        def _():
            rs_out[d] = chunk(ctx_peers[d]).astype(BF16)
            rs_copy(d).start()

    @guarded(c)
    def _():
        total = chunk(c)
        for d in range(1, n_ctx):
            rs_copy(d).wait_recv()
            total = total + rs_in[d].astype(F32)
        low = total.astype(BF16)
        ag_out[...] = low
        for d in range(1, n_ctx):
            ag_copy(d).start()
        gw_ref[:, columns(c)] = low.astype(F32)

    for d in range(1, n_ctx):

        @guarded(ctx_peers[d])
        def _():
            ag_copy(d).wait_recv()
            gw_ref[:, columns(ctx_peers[d])] = ag_in[d].astype(F32)
            rs_copy(d).wait_send()

        @guarded(c)
        def _():
            ag_copy(d).wait_send()

        kv_copies[d].wait_send()
        pk_copies[d].wait_send()
        pv_copies[d].wait_send()
    for e in dk_copies:
        dk_copies[e].wait_send()


def local(n_ctx, n_fsdp, *args):
    queries, keys, features = args[1], args[2], args[7]
    rows = keys.shape[1]
    seqs, _, cols = features.shape
    heads = queries.shape[2] // HEAD_SIZE
    total = HEAD_GROUPS * keys.shape[2]
    reducers = min(n_ctx, HEAD_GROUPS)
    width = total // reducers
    vmem = pl.BlockSpec(memory_space=pltpu.VMEM)
    dma = pltpu.SemaphoreType.DMA
    return pl.pallas_call(
        functools.partial(kernel, n_ctx, n_fsdp, reducers),
        out_shape=(
            jax.ShapeDtypeStruct(queries.shape, BF16),
            jax.ShapeDtypeStruct(keys.shape, BF16),
            jax.ShapeDtypeStruct(keys.shape, BF16),
            jax.ShapeDtypeStruct((cols, total), F32),
        ),
        in_specs=[pl.BlockSpec(memory_space=pltpu.SMEM)] + [vmem] * 7,
        out_specs=(vmem,) * 4,
        scratch_shapes=[
            pltpu.VMEM((n_ctx, 2 * rows + PLACE_ROWS, HEAD_SIZE), BF16),
            pltpu.VMEM((heads * rows, HEAD_SIZE), BF16),
            pltpu.VMEM((heads * rows, HEAD_SIZE), BF16),
            pltpu.VMEM((n_ctx * rows, heads * rows), BF16),
            pltpu.VMEM((n_ctx, rows, HEAD_SIZE), BF16),
            pltpu.VMEM((n_ctx, rows, HEAD_SIZE), BF16),
            pltpu.VMEM((n_ctx, rows, HEAD_SIZE), BF16),
            pltpu.VMEM((n_ctx, rows, HEAD_SIZE), BF16),
            pltpu.VMEM((rows, HEAD_SIZE), F32),
            pltpu.VMEM((rows, HEAD_SIZE), F32),
            pltpu.VMEM((HEAD_GROUPS, seqs * rows, HEAD_SIZE), BF16),
            pltpu.VMEM((cols, seqs * rows), BF16),
            pltpu.VMEM((n_ctx, cols, width), BF16),
            pltpu.VMEM((n_ctx, cols, width), BF16),
            pltpu.VMEM((cols, width), BF16),
            pltpu.VMEM((n_ctx, cols, width), BF16),
        ]
        + [dma((n_ctx,))] * 6
        + [dma((n_fsdp,))] * 2
        + [dma((n_ctx,))] * 4,
        compiler_params=pltpu.CompilerParams(
            collective_id=0, has_side_effects=True, vmem_limit_bytes=40 * 1024 * 1024
        ),
    )(*args)


def solution(mesh):
    return jax.shard_map(
        functools.partial(local, mesh.shape["ctx"], mesh.shape["fsdp"]),
        mesh=mesh,
        in_specs=(
            P(None, "ctx"),
            P("fsdp", "ctx", None),
            P("fsdp", "ctx", None),
            P("fsdp", "ctx", None),
            P("fsdp", "ctx", None),
            P("fsdp", "ctx", None),
            P("fsdp", None, "ctx"),
            P(None, "ctx", "fsdp"),
        ),
        out_specs=(
            P("fsdp", "ctx", None),
            P("fsdp", "ctx", None),
            P("fsdp", "ctx", None),
            P("fsdp", None),
        ),
        check_vma=False,
    )
```

time: 129 us -> 40.7 us (0.32)
  waiting for transfers between devices: 41 us -> 0 us
  Pallas kernels: 0 us -> 32.8 us
  blocking collectives: 29.8 us -> 0 us
  starting transfers between devices: 23 us -> 0 us
  between operations: 14.9 us -> 0.68 us
  matrix products: 5.04 us -> 0 us
  other arithmetic: 3.66 us -> 0 us
  local copies, waits for them, and re-layouts: 9.65 us -> 6.96 us
  loops' own time: 2.07 us -> 0 us
    pallas_call x0 -> x1, Pallas kernels: none -> 32.8 us  [local(): pl.pallas_call(functools.partial(kernel, n_ctx, n_fsdp, reducers), out_sh...]
    all_gather x2 -> x0, blocking collectives: 29.8 us -> none  [the longest x1 15.4 us: local(): grad_wk = lax.all_gather(share, 'ctx', axis=1, tiled=True)]
    ppermute x17 -> x0, starting transfers between devices: 22.9 us -> none  [from_behind(): return lax.ppermute(value, axis, pairs)]
    reduce_scatter x1 -> x0, waiting for transfers between devices: 20.7 us -> none  [local(): share = lax.psum_scatter(summed, 'ctx', scatter_dimension=1, tiled=True)]
    ppermute x17 -> x0, waiting for transfers between devices: 20.4 us -> none  [from_behind(): return lax.ppermute(value, axis, pairs)]
    dot_general x22 -> x0, matrix products: 5.04 us -> none  [the longest x4 1.09 us: block_grads(): jnp.einsum('kgtu,ukd->tkgd', dscores, block_of_keys, preferred_element_ty...]
    add x7 -> x0, other arithmetic: 2.6 us -> none  [the longest x4 2.59 us: block_grads(): query_pos = own_place * query_rows + lax.iota(jnp.int32, query_rows)]
    another operation x1 -> x0, loops' own time: 2.07 us -> none  [local(): lax.fori_loop(0, cycle_length - 1, cycle_step, cycle_state)]
  transfers between devices with their start and end apart: 18 -> 0, of which waited for: 11 -> 0; matrix products, arithmetic and copies ran while one was open for 6% -> 0% of each run, Pallas kernels for 0% -> 0%
where the time goes in v1:
time: 40.7 us; the launch traced here: 40.5 us
  Pallas kernels  32.8 us (81%)
  local copies, waits for them, and re-layouts  6.96 us (17%)
  between operations  0.68 us (2%)
    pallas_call x1, Pallas kernels, local(): pl.pallas_call(functools.partial(kernel, n_ctx, n_fsdp, reducers), out_sh...  32.8 us
    unnamed x17, local copies, waits for them, and re-layouts  6.96 us

profile of v1, /device:TPU:0, one launch (start us, length us, event | category | flops | bytes accessed | tf_op | source)
XLA Modules:
  0.0 40.5 jit_solution(18032775769967562007)
XLA Ops:
  0.6 0.7 %copy.12.pos_ref = s32[2,1]{1,0:T(2,128)S(1)} copy(s32[2,1]{0,1:T(1,128)} %param.8) | data formatting | bytes 16 | tf_op args[0]
  1.4 0.7 %copy.13.lse_ref = f32[1,5,128]{2,1,0:T(8,128)S(1)} copy(f32[1,5,128]{2,0,1:T(1,128)} %param.14) | data formatting | bytes 5120 | tf_op args[6]
  2.1 0.0 copy-start
  2.1 0.0 copy-start.1
  2.1 0.0 copy-start.3
  2.1 1.1 %copy.14.x_ref = bf16[2,128,320]{2,1,0:T(8,128)(2,1)S(1)} copy(bf16[2,128,320]{1,2,0:T(8,128)(2,1)} %param.15) | data formatting | bytes 327680 | tf_op args[7]
  3.2 0.0 copy-done
  3.2 0.0 copy-done.1
  3.2 0.0 copy-done.3
  3.2 0.0 copy-start.2
  3.2 0.9 %copy-done.2 = bf16[1,128,640]{2,1,0:T(8,128)(2,1)S(1)} copy-done((bf16[1,128,640]{2,1,0:T(8,128)(2,1)S(1)}, bf16[1,128,640]{2,1,0:T(8,128)(2,1)}, u32[]{:S(2)}) %copy-start.2) | copy-done | bytes 163864
  4.1 0.0 copy-start.4
  4.1 0.8 %copy-done.4 = bf16[1,128,128]{2,1,0:T(8,128)(2,1)S(1)} copy-done((bf16[1,128,128]{2,1,0:T(8,128)(2,1)S(1)}, bf16[1,128,128]{2,1,0:T(8,128)(2,1)}, u32[]{:S(2)}) %copy-start.4) | copy-done | bytes 32792
  4.9 32.8 %shard_map.111 = (bf16[1,128,640]{2,1,0:T(8,128)(2,1)S(1)}, bf16[1,128,128]{2,1,0:T(8,128)(2,1)S(1)}, bf16[1,128,128]{2,1,0:T(8,128)(2,1)S(1)}, f32[320,512]{1,0:T(8,128)S(1)}) custom-call(s32[2,1]{1,0:T(2,128)S(1)} %copy.12.pos_ref, bf16[1,128,640]{2,1,0:T(8,128)(2,1)S(1)} %copy-done, bf16[1,128,128]{2,1,0:T(8,128)(2,1)S(1)} %copy-done.3, ...), custom_call_target="tpu_custom_call" | custom-call | tf_op jit(solution)/shard_map/pallas_call | solution.py:275
  37.7 0.7 %copy.19 = bf16[1,128,640]{2,1,0:T(8,128)(2,1)} copy(bf16[1,128,640]{2,1,0:T(8,128)(2,1)S(1)} %get-tuple-element.8) | data formatting | bytes 327680
  38.4 0.6 %copy.20 = bf16[1,128,128]{2,1,0:T(8,128)(2,1)} copy(bf16[1,128,128]{2,1,0:T(8,128)(2,1)S(1)} %get-tuple-element.9) | data formatting | bytes 65536
  39.0 0.6 %copy.21 = bf16[1,128,128]{2,1,0:T(8,128)(2,1)} copy(bf16[1,128,128]{2,1,0:T(8,128)(2,1)S(1)} %get-tuple-element.10) | data formatting | bytes 65536
  39.6 0.8 %copy.22 = f32[320,512]{1,0:T(8,128)} copy(f32[320,512]{1,0:T(8,128)S(1)} %get-tuple-element.11) | data formatting | bytes 1310720
Async XLA Ops:
  2.1 1.1 %copy-start = (bf16[1,128,640]{2,1,0:T(8,128)(2,1)S(1)}, bf16[1,128,640]{2,1,0:T(8,128)(2,1)}, u32[]{:S(2)}) copy-start(bf16[1,128,640]{2,1,0:T(8,128)(2,1)} %q_ref.1) | copy-start | bytes 491524
  2.1 1.1 %copy-start.1 = (bf16[1,128,640]{2,1,0:T(8,128)(2,1)S(1)}, bf16[1,128,640]{2,1,0:T(8,128)(2,1)}, u32[]{:S(2)}) copy-start(bf16[1,128,640]{2,1,0:T(8,128)(2,1)} %o_ref.1) | copy-start | bytes 491524
  2.1 1.2 %copy-start.3 = (bf16[1,128,128]{2,1,0:T(8,128)(2,1)S(1)}, bf16[1,128,128]{2,1,0:T(8,128)(2,1)}, u32[]{:S(2)}) copy-start(bf16[1,128,128]{2,1,0:T(8,128)(2,1)} %k_ref.1) | copy-start | bytes 98308
  3.2 0.9 %copy-start.2 = (bf16[1,128,640]{2,1,0:T(8,128)(2,1)S(1)}, bf16[1,128,640]{2,1,0:T(8,128)(2,1)}, u32[]{:S(2)}) copy-start(bf16[1,128,640]{2,1,0:T(8,128)(2,1)} %do_ref.1) | copy-start | bytes 491524
  4.1 0.8 %copy-start.4 = (bf16[1,128,128]{2,1,0:T(8,128)(2,1)S(1)}, bf16[1,128,128]{2,1,0:T(8,128)(2,1)}, u32[]{:S(2)}) copy-start(bf16[1,128,128]{2,1,0:T(8,128)(2,1)} %v_ref.1) | copy-start | bytes 98308

commit v2 on v1

--- a/solution.py
+++ b/solution.py
@@ -74,10 +74,17 @@
     rs_r,
     ag_s,
     ag_r,
+    pos,
+    q_in,
+    do_in,
+    o_in,
+    lse_in,
+    in_s,
 ):
     rows = k_ref.shape[1]
     heads = q_ref.shape[2] // HEAD_SIZE
     seqs = x_ref.shape[0]
+    features = x_ref.shape[1]
     scale = HEAD_SIZE ** (-0.5)
     c = lax.axis_index("ctx")
     f = lax.axis_index("fsdp")
@@ -95,6 +102,20 @@
             device_id_type=pl.DeviceIdType.MESH,
         )
 
+    loads = [
+        (k_ref.at[0], kv.at[0, pl.ds(0, rows)]),
+        (v_ref.at[0], kv.at[0, pl.ds(rows, rows)]),
+        (pos_ref, pos),
+        (do_ref.at[0], do_in),
+        (o_ref.at[0], o_in),
+        (q_ref.at[0], q_in),
+        (lse_ref, lse_in),
+    ]
+    loads += [(x_ref.at[s], x_t.at[:, pl.ds(s * rows, rows)]) for s in range(seqs)]
+    loads = [pltpu.make_async_copy(a, b, in_s.at[i]) for i, (a, b) in enumerate(loads)]
+    for load in loads:
+        load.start()
+
     barrier = pltpu.get_barrier_semaphore()
     for d in range(1, n_ctx):
         pl.semaphore_signal(
@@ -104,9 +125,9 @@
         pl.semaphore_signal(
             barrier, inc=1, device_id=(c, fsdp_peers[e]), device_id_type=pl.DeviceIdType.MESH
         )
-    place = pos_ref[f // HEAD_GROUPS, 0].astype(F32)
-    kv[0, :rows] = k_ref[0]
-    kv[0, rows : 2 * rows] = v_ref[0]
+    for load in loads[:3]:
+        load.wait()
+    place = pos[0, f // HEAD_GROUPS].astype(F32)
     kv[0, 2 * rows :] = jnp.full((PLACE_ROWS, HEAD_SIZE), place, F32).astype(BF16)
     pl.semaphore_wait(barrier, n_ctx - 1 + len(direct))
 
@@ -115,16 +136,17 @@
         kv_copies[d] = remote(kv.at[0], kv.at[d], kv_s.at[d], kv_r.at[d], (ctx_peers[d], f))
         kv_copies[d].start()
 
+    for load in loads[3:7]:
+        load.wait()
     delta = []
     for h in range(heads):
         cols = slice(h * HEAD_SIZE, (h + 1) * HEAD_SIZE)
-        qs[h * rows : (h + 1) * rows] = q_ref[0, :, cols]
-        dos[h * rows : (h + 1) * rows] = do_ref[0, :, cols]
-        product = do_ref[0, :, cols].astype(F32) * o_ref[0, :, cols].astype(F32)
+        qs[h * rows : (h + 1) * rows] = q_in[:, cols]
+        dos[h * rows : (h + 1) * rows] = do_in[:, cols]
+        product = do_in[:, cols].astype(F32) * o_in[:, cols].astype(F32)
         delta.append(jnp.sum(product.T, axis=0, keepdims=True))
     delta = jnp.concatenate(delta, axis=1)
-    norms = lse_ref[0]
-    norm = jnp.concatenate([norms[h : h + 1] for h in range(heads)], axis=1)
+    norm = jnp.concatenate([lse_in[h] for h in range(heads)], axis=1)
     token = lax.broadcasted_iota(jnp.int32, (1, rows), 1).astype(F32)
     key_row = lax.broadcasted_iota(jnp.int32, (rows, heads * rows), 0).astype(F32)
 
@@ -144,8 +166,6 @@
     own_k, own_v = visit(0)
     acc_k[...] = own_k
     acc_v[...] = own_v()
-    for s in range(seqs):
-        x_t[:, s * rows : (s + 1) * rows] = x_ref[s].T
 
     pk_copies, pv_copies = {}, {}
     for d in range(1, n_ctx):
@@ -191,6 +211,67 @@
         there = slot(fsdp_peers[e])
         remote(there, there, dk_s.at[e], dk_r.at[e], (c, fsdp_peers[1])).wait_recv()
 
+    for load in loads[7:]:
+        load.wait()
+    part = features // reducers
+    half = HEAD_GROUPS // 2
+    parity = lax.rem(f, 2)
+
+    def rs_copy(p, d):
+        i = p * n_ctx + d
+        return remote(rs_out.at[p, ctx_peers[d]], rs_in.at[p, d], rs_s.at[i], rs_r.at[i], (ctx_peers[d], f))
+
+    def ag_copy(p, d):
+        i = p * n_ctx + d
+        return remote(ag_out.at[p], ag_in.at[p, d], ag_s.at[i], ag_r.at[i], (ctx_peers[d], f))
+
+    def when_reducer(index, body):
+        if reducers == n_ctx:
+            body()
+        else:
+            pl.when(index < reducers)(body)
+
+    def group(p, j):
+        return 2 * j + lax.rem(parity + p, 2)
+
+    def spread(p):
+        for j in range(half):
+            sums = dot(x_t[...], dk_all[group(p, j)], (1, 0))
+            for owner in range(reducers):
+                rs_out[p, owner, j] = sums[owner * part : (owner + 1) * part].astype(BF16)
+        for d in range(1, n_ctx):
+            when_reducer(ctx_peers[d], lambda: rs_copy(p, d).start())
+
+    def store(p, owner, pieces):
+        for j in range(half):
+            at = pl.ds(pl.multiple_of(owner * part, 8), part)
+            columns = pl.ds(pl.multiple_of(group(p, j) * HEAD_SIZE, HEAD_SIZE), HEAD_SIZE)
+            gw_ref[at, columns] = pieces[j].astype(F32)
+
+    def reduce(p):
+        def body():
+            for d in range(1, n_ctx):
+                rs_copy(p, d).wait_recv()
+            for j in range(half):
+                total = rs_out[p, c, j].astype(F32)
+                for d in range(1, n_ctx):
+                    total = total + rs_in[p, d, j].astype(F32)
+                ag_out[p, j] = total.astype(BF16)
+            for d in range(1, n_ctx):
+                ag_copy(p, d).start()
+            store(p, c, ag_out[p])
+
+        when_reducer(c, body)
+
+    def collect(p):
+        for d in range(1, n_ctx):
+
+            def body():
+                ag_copy(p, d).wait_recv()
+                store(p, ctx_peers[d], ag_in[p, d])
+
+            when_reducer(ctx_peers[d], body)
+
     for e in direct[1:]:
         arrived(e)
         there = slot(fsdp_peers[e])
@@ -198,63 +279,20 @@
             there, there, dk_s.at[e + 1], dk_r.at[e + 1], (c, fsdp_peers[1])
         )
         dk_copies[e + 1].start()
+    spread(0)
     arrived(1)
     for e in direct[1:]:
         arrived(e + 1)
-
-    width = gw_ref.shape[1] // reducers
-
-    def chunk(owner):
-        per = HEAD_SIZE
-        groups = width // per
-        parts = [dot(x_t[...], dk_all[owner * groups + g], (1, 0)) for g in range(groups)]
-        return parts[0] if groups == 1 else jnp.concatenate(parts, axis=1)
-
-    def columns(owner):
-        return pl.ds(pl.multiple_of(owner * width, width), width)
-
-    def guarded(index):
-        if reducers == n_ctx:
-            return lambda body: body()
-        return pl.when(index < reducers)
-
-    def rs_copy(d):
-        return remote(rs_out.at[d], rs_in.at[d], rs_s.at[d], rs_r.at[d], (ctx_peers[d], f))
-
-    def ag_copy(d):
-        return remote(ag_out, ag_in.at[d], ag_s.at[d], ag_r.at[d], (ctx_peers[d], f))
-
-    for d in range(1, n_ctx):
-
-        @guarded(ctx_peers[d])
-        def _():
-            rs_out[d] = chunk(ctx_peers[d]).astype(BF16)
-            rs_copy(d).start()
-
-    @guarded(c)
-    def _():
-        total = chunk(c)
-        for d in range(1, n_ctx):
-            rs_copy(d).wait_recv()
-            total = total + rs_in[d].astype(F32)
-        low = total.astype(BF16)
-        ag_out[...] = low
-        for d in range(1, n_ctx):
-            ag_copy(d).start()
-        gw_ref[:, columns(c)] = low.astype(F32)
-
-    for d in range(1, n_ctx):
-
-        @guarded(ctx_peers[d])
-        def _():
-            ag_copy(d).wait_recv()
-            gw_ref[:, columns(ctx_peers[d])] = ag_in[d].astype(F32)
-            rs_copy(d).wait_send()
-
-        @guarded(c)
-        def _():
-            ag_copy(d).wait_send()
-
+    spread(1)
+    reduce(0)
+    reduce(1)
+    collect(0)
+    collect(1)
+
+    for d in range(1, n_ctx):
+        for p in range(2):
+            when_reducer(ctx_peers[d], lambda: rs_copy(p, d).wait_send())
+            when_reducer(c, lambda: ag_copy(p, d).wait_send())
         kv_copies[d].wait_send()
         pk_copies[d].wait_send()
         pv_copies[d].wait_send()
@@ -262,25 +300,35 @@
         dk_copies[e].wait_send()
 
 
-def local(n_ctx, n_fsdp, *args):
-    queries, keys, features = args[1], args[2], args[7]
+def write_out(*refs):
+    count = len(refs) // 2
+    for i in range(count):
+        refs[count + i][...] = refs[i][...]
+
+
+def local(
+    n_ctx, n_fsdp, block_pos, queries, keys, values, output, output_gradient, norm, features
+):
     rows = keys.shape[1]
     seqs, _, cols = features.shape
     heads = queries.shape[2] // HEAD_SIZE
     total = HEAD_GROUPS * keys.shape[2]
-    reducers = min(n_ctx, HEAD_GROUPS)
-    width = total // reducers
+    reducers = max(r for r in range(1, n_ctx + 1) if cols % (16 * r) == 0)
+    part = cols // reducers
+    half = HEAD_GROUPS // 2
     vmem = pl.BlockSpec(memory_space=pltpu.VMEM)
+    hbm = pl.BlockSpec(memory_space=pltpu.HBM)
     dma = pltpu.SemaphoreType.DMA
-    return pl.pallas_call(
+    shapes = (
+        jax.ShapeDtypeStruct(queries.shape, BF16),
+        jax.ShapeDtypeStruct(keys.shape, BF16),
+        jax.ShapeDtypeStruct(keys.shape, BF16),
+        jax.ShapeDtypeStruct((cols, total), F32),
+    )
+    results = pl.pallas_call(
         functools.partial(kernel, n_ctx, n_fsdp, reducers),
-        out_shape=(
-            jax.ShapeDtypeStruct(queries.shape, BF16),
-            jax.ShapeDtypeStruct(keys.shape, BF16),
-            jax.ShapeDtypeStruct(keys.shape, BF16),
-            jax.ShapeDtypeStruct((cols, total), F32),
-        ),
-        in_specs=[pl.BlockSpec(memory_space=pltpu.SMEM)] + [vmem] * 7,
+        out_shape=shapes,
+        in_specs=[hbm] * 8,
         out_specs=(vmem,) * 4,
         scratch_shapes=[
             pltpu.VMEM((n_ctx, 2 * rows + PLACE_ROWS, HEAD_SIZE), BF16),
@@ -295,18 +343,41 @@
             pltpu.VMEM((rows, HEAD_SIZE), F32),
             pltpu.VMEM((HEAD_GROUPS, seqs * rows, HEAD_SIZE), BF16),
             pltpu.VMEM((cols, seqs * rows), BF16),
-            pltpu.VMEM((n_ctx, cols, width), BF16),
-            pltpu.VMEM((n_ctx, cols, width), BF16),
-            pltpu.VMEM((cols, width), BF16),
-            pltpu.VMEM((n_ctx, cols, width), BF16),
+            pltpu.VMEM((2, n_ctx, half, part, HEAD_SIZE), BF16),
+            pltpu.VMEM((2, n_ctx, half, part, HEAD_SIZE), BF16),
+            pltpu.VMEM((2, half, part, HEAD_SIZE), BF16),
+            pltpu.VMEM((2, n_ctx, half, part, HEAD_SIZE), BF16),
         ]
         + [dma((n_ctx,))] * 6
         + [dma((n_fsdp,))] * 2
-        + [dma((n_ctx,))] * 4,
+        + [dma((2 * n_ctx,))] * 4
+        + [
+            pltpu.SMEM((1, seqs), jnp.int32),
+            pltpu.VMEM(queries.shape[1:], BF16),
+            pltpu.VMEM(queries.shape[1:], BF16),
+            pltpu.VMEM(queries.shape[1:], BF16),
+            pltpu.VMEM((heads, 1, rows), F32),
+            dma((7 + seqs,)),
+        ],
         compiler_params=pltpu.CompilerParams(
-            collective_id=0, has_side_effects=True, vmem_limit_bytes=40 * 1024 * 1024
+            collective_id=0, has_side_effects=True, vmem_limit_bytes=60 * 1024 * 1024
         ),
-    )(*args)
+    )(
+        block_pos.T,
+        queries,
+        keys,
+        values,
+        output,
+        output_gradient,
+        jnp.swapaxes(norm, 0, 1),
+        jnp.swapaxes(features, 1, 2),
+    )
+    return pl.pallas_call(
+        write_out,
+        out_shape=shapes,
+        in_specs=[vmem] * 4,
+        out_specs=(vmem,) * 4,
+    )(*results)
 
 
 def solution(mesh):

time: 40.7 us -> 34.2 us (0.84)
  local copies, waits for them, and re-layouts: 6.96 us -> 0 us
  Pallas kernels: 32.8 us -> 33.4 us
    unnamed x17 -> x0, local copies, waits for them, and re-layouts: 6.96 us -> none
    pallas_call x0 -> x1, Pallas kernels: none -> 2.14 us  [local(): pl.pallas_call(write_out, out_shape=shapes, in_specs=[vmem] * 4, out_spec...]
    pallas_call x1, Pallas kernels: 32.8 us -> 31.3 us  [local(): pl.pallas_call(functools.partial(kernel, n_ctx, n_fsdp, reducers), out_sh...]
where the time goes in v2:
time: 34.2 us; the launch traced here: 34.1 us
  Pallas kernels  33.4 us (98%)
  between operations  0.64 us (2%)
    pallas_call x1, Pallas kernels, local(): pl.pallas_call(functools.partial(kernel, n_ctx, n_fsdp, reducers), out_sh...  31.3 us
    pallas_call x1, Pallas kernels, local(): pl.pallas_call(write_out, out_shape=shapes, in_specs=[vmem] * 4, out_spec...  2.14 us

profile of v2, /device:TPU:0, one launch (start us, length us, event | category | flops | bytes accessed | tf_op | source)
XLA Modules:
  0.0 34.1 jit_solution(13228427356408033700)
XLA Ops:
  0.6 31.3 %shard_map.111 = (bf16[1,128,640]{2,1,0:T(8,128)(2,1)}, bf16[1,128,128]{2,1,0:T(8,128)(2,1)}, bf16[1,128,128]{2,1,0:T(8,128)(2,1)}, f32[320,512]{1,0:T(8,128)}) custom-call(s32[1,2]{1,0:T(1,128)} %bitcast.5, bf16[1,128,640]{2,1,0:T(8,128)(2,1)} %q_ref.1, bf16[1,128,128]{2,1,0:T(8,128)(2,1)} %k_ref.1, bf16[1,128,128]{2,1,0:T(8,128)(2,1)} %v_ref.1, ...), custom_call_target="tpu_custom_call" | custom-call | tf_op jit(solution)/shard_map/pallas_call | solution.py:328
  31.9 2.1 %shard_map.112 = (bf16[1,128,640]{2,1,0:T(8,128)(2,1)}, bf16[1,128,128]{2,1,0:T(8,128)(2,1)}, bf16[1,128,128]{2,1,0:T(8,128)(2,1)}, f32[320,512]{1,0:T(8,128)}) custom-call(bf16[1,128,640]{2,1,0:T(8,128)(2,1)} %get-tuple-element.8.refs_0_, bf16[1,128,128]{2,1,0:T(8,128)(2,1)} %get-tuple-element.9.refs_1_, bf16[1,128,128]{2,1,0:T(8,128)(2,1)} %get-tuple-element.10.refs_2_, ...), custom_call_target="tpu_custom_call" | custom-call | tf_op jit(solution)/shard_map/pallas_call | solution.py:375

commit v3 on v2

--- a/solution.py
+++ b/solution.py
@@ -42,10 +42,10 @@
     do_ref,
     lse_ref,
     x_ref,
-    gq_ref,
-    gk_ref,
-    gv_ref,
-    gw_ref,
+    gq_out,
+    gk_out,
+    gv_out,
+    gw_out,
     kv,
     qs,
     dos,
@@ -61,7 +61,6 @@
     rs_out,
     rs_in,
     ag_out,
-    ag_in,
     kv_s,
     kv_r,
     pk_s,
@@ -80,6 +79,11 @@
     o_in,
     lse_in,
     in_s,
+    gq_ref,
+    gk_ref,
+    gv_ref,
+    ps,
+    out_s,
 ):
     rows = k_ref.shape[1]
     heads = q_ref.shape[2] // HEAD_SIZE
@@ -102,6 +106,15 @@
             device_id_type=pl.DeviceIdType.MESH,
         )
 
+    barrier = pltpu.get_barrier_semaphore()
+    for d in range(1, n_ctx):
+        pl.semaphore_signal(
+            barrier, inc=1, device_id=(ctx_peers[d], f), device_id_type=pl.DeviceIdType.MESH
+        )
+    for e in direct:
+        pl.semaphore_signal(
+            barrier, inc=1, device_id=(c, fsdp_peers[e]), device_id_type=pl.DeviceIdType.MESH
+        )
     loads = [
         (k_ref.at[0], kv.at[0, pl.ds(0, rows)]),
         (v_ref.at[0], kv.at[0, pl.ds(rows, rows)]),
@@ -116,15 +129,10 @@
     for load in loads:
         load.start()
 
-    barrier = pltpu.get_barrier_semaphore()
-    for d in range(1, n_ctx):
-        pl.semaphore_signal(
-            barrier, inc=1, device_id=(ctx_peers[d], f), device_id_type=pl.DeviceIdType.MESH
-        )
-    for e in direct:
-        pl.semaphore_signal(
-            barrier, inc=1, device_id=(c, fsdp_peers[e]), device_id_type=pl.DeviceIdType.MESH
-        )
+    writes = [
+        pltpu.make_async_copy(a, b, out_s.at[i])
+        for i, (a, b) in enumerate([(gq_ref, gq_out), (gk_ref, gk_out), (gv_ref, gv_out)])
+    ]
     for load in loads[:3]:
         load.wait()
     place = pos[0, f // HEAD_GROUPS].astype(F32)
@@ -161,28 +169,36 @@
         dprobs = dot(value, dos[...], (1, 1))
         dscores = (probs * (dprobs - delta) * scale).astype(BF16)
         ds[d * rows : (d + 1) * rows] = dscores
-        return dot(dscores, qs[...], (1, 0)), lambda: dot(probs.astype(BF16), dos[...], (1, 0))
-
-    own_k, own_v = visit(0)
-    acc_k[...] = own_k
-    acc_v[...] = own_v()
+        ps[d * rows : (d + 1) * rows] = probs.astype(BF16)
+        return dot(dscores, qs[...], (1, 0))
+
+    def value_part(d):
+        return dot(ps[d * rows : (d + 1) * rows], dos[...], (1, 0))
+
+    acc_k[...] = visit(0)
 
     pk_copies, pv_copies = {}, {}
     for d in range(1, n_ctx):
         kv_copies[d].wait_recv()
-        to_k, to_v = visit(d)
-        device = (ctx_peers[d], f)
-        part_k[d] = to_k.astype(BF16)
-        pk_copies[d] = remote(part_k.at[d], got_k.at[d], pk_s.at[d], pk_r.at[d], device)
+        part_k[d] = visit(d).astype(BF16)
+        pk_copies[d] = remote(
+            part_k.at[d], got_k.at[d], pk_s.at[d], pk_r.at[d], (ctx_peers[d], f)
+        )
         pk_copies[d].start()
-        part_v[d] = to_v().astype(BF16)
-        pv_copies[d] = remote(part_v.at[d], got_v.at[d], pv_s.at[d], pv_r.at[d], device)
+    for d in range(1, n_ctx):
+        part_v[d] = value_part(d).astype(BF16)
+        pv_copies[d] = remote(
+            part_v.at[d], got_v.at[d], pv_s.at[d], pv_r.at[d], (ctx_peers[d], f)
+        )
         pv_copies[d].start()
+    acc_v[...] = value_part(0)
 
     keys_all = jnp.concatenate([kv[d, :rows] for d in range(n_ctx)], axis=0)
     for h in range(heads):
         cols = slice(h * HEAD_SIZE, (h + 1) * HEAD_SIZE)
         gq_ref[0, :, cols] = dot(ds[:, cols], keys_all, (0, 0)).astype(BF16)
+
+    writes[0].start()
 
     dk = acc_k[...]
     for d in range(1, n_ctx):
@@ -201,11 +217,13 @@
     for e in direct:
         dk_copies[e] = remote(own_slot, own_slot, dk_s.at[e], dk_r.at[e], (c, fsdp_peers[e]))
         dk_copies[e].start()
+    writes[1].start()
     dv = acc_v[...]
     for d in range(1, n_ctx):
         pv_copies[d].wait_recv()
         dv = dv + got_v[d].astype(F32)
     gv_ref[0] = dv.astype(BF16)
+    writes[2].start()
 
     def arrived(e):
         there = slot(fsdp_peers[e])
@@ -221,9 +239,17 @@
         i = p * n_ctx + d
         return remote(rs_out.at[p, ctx_peers[d]], rs_in.at[p, d], rs_s.at[i], rs_r.at[i], (ctx_peers[d], f))
 
-    def ag_copy(p, d):
+    def region(p, owner):
+        at = pl.ds(pl.multiple_of(owner * part, 16), part)
+        return gw_out.at[lax.rem(parity + p, 2), :, at]
+
+    def ag_copy(p, d, owner):
         i = p * n_ctx + d
-        return remote(ag_out.at[p], ag_in.at[p, d], ag_s.at[i], ag_r.at[i], (ctx_peers[d], f))
+        place_of = region(p, owner)
+        return remote(ag_out.at[p], place_of, ag_s.at[i], ag_r.at[i], (ctx_peers[d], f))
+
+    def own_copy(p):
+        return pltpu.make_async_copy(ag_out.at[p], region(p, c), out_s.at[3 + p])
 
     def when_reducer(index, body):
         if reducers == n_ctx:
@@ -241,12 +267,6 @@
                 rs_out[p, owner, j] = sums[owner * part : (owner + 1) * part].astype(BF16)
         for d in range(1, n_ctx):
             when_reducer(ctx_peers[d], lambda: rs_copy(p, d).start())
-
-    def store(p, owner, pieces):
-        for j in range(half):
-            at = pl.ds(pl.multiple_of(owner * part, 8), part)
-            columns = pl.ds(pl.multiple_of(group(p, j) * HEAD_SIZE, HEAD_SIZE), HEAD_SIZE)
-            gw_ref[at, columns] = pieces[j].astype(F32)
 
     def reduce(p):
         def body():
@@ -258,19 +278,16 @@
                     total = total + rs_in[p, d, j].astype(F32)
                 ag_out[p, j] = total.astype(BF16)
             for d in range(1, n_ctx):
-                ag_copy(p, d).start()
-            store(p, c, ag_out[p])
+                ag_copy(p, d, c).start()
+            own_copy(p).start()
 
         when_reducer(c, body)
 
     def collect(p):
         for d in range(1, n_ctx):
-
-            def body():
-                ag_copy(p, d).wait_recv()
-                store(p, ctx_peers[d], ag_in[p, d])
-
-            when_reducer(ctx_peers[d], body)
+            when_reducer(
+                ctx_peers[d], lambda: ag_copy(p, d, ctx_peers[d]).wait_recv()
+            )
 
     for e in direct[1:]:
         arrived(e)
@@ -292,18 +309,38 @@
     for d in range(1, n_ctx):
         for p in range(2):
             when_reducer(ctx_peers[d], lambda: rs_copy(p, d).wait_send())
-            when_reducer(c, lambda: ag_copy(p, d).wait_send())
+            when_reducer(c, lambda: ag_copy(p, d, c).wait_send())
         kv_copies[d].wait_send()
         pk_copies[d].wait_send()
         pv_copies[d].wait_send()
     for e in dk_copies:
         dk_copies[e].wait_send()
+    for write in writes:
+        write.wait()
+    for p in range(2):
+        when_reducer(c, lambda: own_copy(p).wait())
 
 
 def write_out(*refs):
-    count = len(refs) // 2
-    for i in range(count):
-        refs[count + i][...] = refs[i][...]
+    sources, targets, held = refs[:4], refs[4:8], refs[8:12]
+    wide, in_s, out_s = refs[12:]
+    loads = [pltpu.make_async_copy(sources[i], held[i], in_s.at[i]) for i in range(4)]
+    stores = [
+        pltpu.make_async_copy(wide if i == 3 else held[i], targets[i], out_s.at[i])
+        for i in range(4)
+    ]
+    for i in (3, 0, 1, 2):
+        loads[i].start()
+    for i in range(3):
+        loads[i].wait()
+        stores[i].start()
+    loads[3].wait()
+    for group in range(HEAD_GROUPS):
+        columns = slice(group * HEAD_SIZE, (group + 1) * HEAD_SIZE)
+        wide[:, columns] = held[3][group % 2, group // 2].astype(F32)
+    stores[3].start()
+    for store in stores:
+        store.wait()
 
 
 def local(
@@ -316,20 +353,19 @@
     reducers = max(r for r in range(1, n_ctx + 1) if cols % (16 * r) == 0)
     part = cols // reducers
     half = HEAD_GROUPS // 2
-    vmem = pl.BlockSpec(memory_space=pltpu.VMEM)
     hbm = pl.BlockSpec(memory_space=pltpu.HBM)
     dma = pltpu.SemaphoreType.DMA
     shapes = (
         jax.ShapeDtypeStruct(queries.shape, BF16),
         jax.ShapeDtypeStruct(keys.shape, BF16),
         jax.ShapeDtypeStruct(keys.shape, BF16),
-        jax.ShapeDtypeStruct((cols, total), F32),
+        jax.ShapeDtypeStruct((2, half, cols, HEAD_SIZE), BF16),
     )
     results = pl.pallas_call(
         functools.partial(kernel, n_ctx, n_fsdp, reducers),
         out_shape=shapes,
         in_specs=[hbm] * 8,
-        out_specs=(vmem,) * 4,
+        out_specs=(hbm,) * 4,
         scratch_shapes=[
             pltpu.VMEM((n_ctx, 2 * rows + PLACE_ROWS, HEAD_SIZE), BF16),
             pltpu.VMEM((heads * rows, HEAD_SIZE), BF16),
@@ -346,7 +382,6 @@
             pltpu.VMEM((2, n_ctx, half, part, HEAD_SIZE), BF16),
             pltpu.VMEM((2, n_ctx, half, part, HEAD_SIZE), BF16),
             pltpu.VMEM((2, half, part, HEAD_SIZE), BF16),
-            pltpu.VMEM((2, n_ctx, half, part, HEAD_SIZE), BF16),
         ]
         + [dma((n_ctx,))] * 6
         + [dma((n_fsdp,))] * 2
@@ -358,6 +393,11 @@
             pltpu.VMEM(queries.shape[1:], BF16),
             pltpu.VMEM((heads, 1, rows), F32),
             dma((7 + seqs,)),
+            pltpu.VMEM(queries.shape, BF16),
+            pltpu.VMEM(keys.shape, BF16),
+            pltpu.VMEM(keys.shape, BF16),
+            pltpu.VMEM((n_ctx * rows, heads * rows), BF16),
+            dma((5,)),
         ],
         compiler_params=pltpu.CompilerParams(
             collective_id=0, has_side_effects=True, vmem_limit_bytes=60 * 1024 * 1024
@@ -374,9 +414,11 @@
     )
     return pl.pallas_call(
         write_out,
-        out_shape=shapes,
-        in_specs=[vmem] * 4,
-        out_specs=(vmem,) * 4,
+        out_shape=(*shapes[:3], jax.ShapeDtypeStruct((cols, total), F32)),
+        in_specs=[hbm] * 4,
+        out_specs=(hbm,) * 4,
+        scratch_shapes=[pltpu.VMEM(each.shape, each.dtype) for each in shapes]
+        + [pltpu.VMEM((cols, total), F32), dma((4,)), dma((4,))],
     )(*results)
 
 

time: 34.2 us -> 33.1 us (0.968)
  Pallas kernels: 33.4 us -> 32.3 us
    pallas_call x1, Pallas kernels: 31.3 us -> 30.3 us  [local(): pl.pallas_call(functools.partial(kernel, n_ctx, n_fsdp, reducers), out_sh...]
where the time goes in v3:
time: 33.1 us; the launch traced here: 32.9 us
  Pallas kernels  32.3 us (98%)
  between operations  0.64 us (2%)
    pallas_call x1, Pallas kernels, local(): pl.pallas_call(functools.partial(kernel, n_ctx, n_fsdp, reducers), out_sh...  30.3 us
    pallas_call x1, Pallas kernels, local(): pl.pallas_call(write_out, out_shape=(*shapes[:3], jax.ShapeDtypeStruct((c...  2.01 us

profile of v3, /device:TPU:0, one launch (start us, length us, event | category | flops | bytes accessed | tf_op | source)
XLA Modules:
  0.0 32.9 jit_solution(2072034289486526641)
XLA Ops:
  0.6 30.3 %shard_map.111 = (bf16[1,128,640]{2,1,0:T(8,128)(2,1)}, bf16[1,128,128]{2,1,0:T(8,128)(2,1)}, bf16[1,128,128]{2,1,0:T(8,128)(2,1)}, bf16[2,2,320,128]{3,2,1,0:T(8,128)(2,1)}) custom-call(s32[1,2]{1,0:T(1,128)} %bitcast.5, bf16[1,128,640]{2,1,0:T(8,128)(2,1)} %q_ref.1, bf16[1,128,128]{2,1,0:T(8,128)(2,1)} %k_ref.1, bf16[1,128,128]{2,1,0:T(8,128)(2,1)} %v_ref.1, ...), custom_call_target="tpu_custom_call" | custom-call | tf_op jit(solution)/shard_map/pallas_call | solution.py:364
  30.9 2.0 %shard_map.112 = (bf16[1,128,640]{2,1,0:T(8,128)(2,1)}, bf16[1,128,128]{2,1,0:T(8,128)(2,1)}, bf16[1,128,128]{2,1,0:T(8,128)(2,1)}, f32[320,512]{1,0:T(8,128)}) custom-call(bf16[1,128,640]{2,1,0:T(8,128)(2,1)} %get-tuple-element.8.refs_0_, bf16[1,128,128]{2,1,0:T(8,128)(2,1)} %get-tuple-element.9.refs_1_, bf16[1,128,128]{2,1,0:T(8,128)(2,1)} %get-tuple-element.10.refs_2_, ...), custom_call_target="tpu_custom_call" | custom-call | tf_op jit(solution)/shard_map/pallas_call | solution.py:415

commit v4 on v3

--- a/solution.py
+++ b/solution.py
@@ -140,7 +140,7 @@
     pl.semaphore_wait(barrier, n_ctx - 1 + len(direct))
 
     kv_copies = {}
-    for d in range(1, n_ctx):
+    for d in reversed(range(1, n_ctx)):
         kv_copies[d] = remote(kv.at[0], kv.at[d], kv_s.at[d], kv_r.at[d], (ctx_peers[d], f))
         kv_copies[d].start()
 
@@ -214,7 +214,7 @@
     own_slot = slot(f)
     own_slot[...] = dk_low
     dk_copies = {}
-    for e in direct:
+    for e in reversed(direct):
         dk_copies[e] = remote(own_slot, own_slot, dk_s.at[e], dk_r.at[e], (c, fsdp_peers[e]))
         dk_copies[e].start()
     writes[1].start()
@@ -265,7 +265,7 @@
             sums = dot(x_t[...], dk_all[group(p, j)], (1, 0))
             for owner in range(reducers):
                 rs_out[p, owner, j] = sums[owner * part : (owner + 1) * part].astype(BF16)
-        for d in range(1, n_ctx):
+        for d in reversed(range(1, n_ctx)):
             when_reducer(ctx_peers[d], lambda: rs_copy(p, d).start())
 
     def reduce(p):
@@ -277,7 +277,7 @@
                 for d in range(1, n_ctx):
                     total = total + rs_in[p, d, j].astype(F32)
                 ag_out[p, j] = total.astype(BF16)
-            for d in range(1, n_ctx):
+            for d in reversed(range(1, n_ctx)):
                 ag_copy(p, d, c).start()
             own_copy(p).start()
 

time: 33.1 us -> 32 us (0.967)
  Pallas kernels: 32.3 us -> 31.2 us
    pallas_call x1, Pallas kernels: 30.3 us -> 29.2 us  [local(): pl.pallas_call(functools.partial(kernel, n_ctx, n_fsdp, reducers), out_sh...]
where the time goes in v4:
time: 32 us; the launch traced here: 31.9 us
  Pallas kernels  31.2 us (98%)
  between operations  0.64 us (2%)
    pallas_call x1, Pallas kernels, local(): pl.pallas_call(functools.partial(kernel, n_ctx, n_fsdp, reducers), out_sh...  29.2 us
    pallas_call x1, Pallas kernels, local(): pl.pallas_call(write_out, out_shape=(*shapes[:3], jax.ShapeDtypeStruct((c...  2.01 us

profile of v4, /device:TPU:0, one launch (start us, length us, event | category | flops | bytes accessed | tf_op | source)
XLA Modules:
  0.0 31.9 jit_solution(15230576261484024645)
XLA Ops:
  0.6 29.2 %shard_map.111 = (bf16[1,128,640]{2,1,0:T(8,128)(2,1)}, bf16[1,128,128]{2,1,0:T(8,128)(2,1)}, bf16[1,128,128]{2,1,0:T(8,128)(2,1)}, bf16[2,2,320,128]{3,2,1,0:T(8,128)(2,1)}) custom-call(s32[1,2]{1,0:T(1,128)} %bitcast.5, bf16[1,128,640]{2,1,0:T(8,128)(2,1)} %q_ref.1, bf16[1,128,128]{2,1,0:T(8,128)(2,1)} %k_ref.1, bf16[1,128,128]{2,1,0:T(8,128)(2,1)} %v_ref.1, ...), custom_call_target="tpu_custom_call" | custom-call | tf_op jit(solution)/shard_map/pallas_call | solution.py:364
  29.8 2.0 %shard_map.112 = (bf16[1,128,640]{2,1,0:T(8,128)(2,1)}, bf16[1,128,128]{2,1,0:T(8,128)(2,1)}, bf16[1,128,128]{2,1,0:T(8,128)(2,1)}, f32[320,512]{1,0:T(8,128)}) custom-call(bf16[1,128,640]{2,1,0:T(8,128)(2,1)} %get-tuple-element.8.refs_0_, bf16[1,128,128]{2,1,0:T(8,128)(2,1)} %get-tuple-element.9.refs_1_, bf16[1,128,128]{2,1,0:T(8,128)(2,1)} %get-tuple-element.10.refs_2_, ...), custom_call_target="tpu_custom_call" | custom-call | tf_op jit(solution)/shard_map/pallas_call | solution.py:415
